TPU v7x, 512 devices: a whole 4x4x16 slice. The times are simulated.
512 devices in a mesh: dp: 32 (over z, core), seq: 16 (over y, x).
Axes of the slice: x: 4, y: 4, z: 16, core: 2. Of those that a mesh axis runs over, the one named last changes fastest.
Arguments:
- features: bfloat16 [262144, 1536], P(('dp', 'seq')), parts along dimension 0, may hold values from -6 to 6
- conv_taps: float32 [5, 1536], replicated, may hold values from -2.5 to 2.5
- norm_gain: float32 [1536], replicated, may hold values from 0.5 to 2
- point_weight: bfloat16 [1536, 1536], replicated, may hold values from -0.15625 to 0.15625
- donor_weight: bfloat16 [1536, 768], replicated, may hold values from -0.15625 to 0.15625
- accept_weight: bfloat16 [1536, 768], replicated, may hold values from -0.15625 to 0.15625
- donor_pos: int32 [32768], P(('dp', 'seq')), parts along dimension 0, may hold values from 0 to 8191, as said below
- accept_pos: int32 [32768], P(('dp', 'seq')), parts along dimension 0, may hold values from 0 to 8191, as said below
- pair_counts: int32 [512], P(('dp', 'seq')), parts along dimension 0, may hold values from 1 to 64, 512 in all
Outputs:
- encoded: bfloat16 [262144, 1536], P(('dp', 'seq')), parts along dimension 0
- junction: bfloat16 [32768, 768], P(('dp', 'seq')), parts along dimension 0
There are 32 independent parts, one for each index of `dp`. A program takes and returns all parts, laid end to end along the dimension named above; an argument that names none is the same for every part. Nothing has to cross between parts.
Inputs may be any that keep to these rules, and one draw needn't show every extreme that they name: `pair_counts`: the live counts sum to 512 and the largest is exactly 64. `donor_pos`: among the 128 donor and acceptor positions of the slots s * 64 to s * 64 + 63, at most 16 lie in any one block of 512 positions r * 512 to r * 512 + 511, and exactly 16 lie in one such block. `accept_pos`: as for donor_pos, with the two lists counted together.
All inputs are finite; a program needn't handle non-finite values. No bound on the sum of `pair_counts` on one device may be relied on, other than what follows from the above.
Results may differ from a plain program's by a relative error of at most 0.0064.
Values may be sent and summed in bfloat16 or wider, within the bound.
A program may use at most 128 MiB of HBM per device.

v0:
```python
import jax
import jax.numpy as jnp
from jax import lax
from jax.sharding import PartitionSpec as P


def padded_2(array, sides, width):
    for axis, dim in sides:
        size, length = (lax.axis_size(axis), array.shape[dim])
        up = [(i, (i + 1) % size) for i in range(size - 1)]
        down = [(j, i) for i, j in up]
        last = lax.slice_in_dim(array, length - width, length, axis=dim)
        leading = lax.slice_in_dim(array, 0, width, axis=dim)
        before = lax.ppermute(last, axis, up)
        after = lax.ppermute(leading, axis, down)
        array = jnp.concatenate([before, array, after], axis=dim)
    return array


def on_device(
    features,
    conv_taps,
    norm_gain,
    point_weight,
    donor_weight,
    accept_weight,
    donor_pos,
    accept_pos,
    pair_counts,
):
    rows = features.shape[0]
    slots = donor_pos.shape[0]
    padded = padded_2(features, (("seq", 0),), 2).astype(jnp.float32)
    conv = conv_taps[0][None, :] * padded[0:rows]
    for k in range(1, conv_taps.shape[0]):
        conv = conv + conv_taps[k][None, :] * padded[k : k + rows]
    scale = lax.rsqrt(jnp.mean(conv * conv, axis=-1, keepdims=True) + 1e-06)
    normed = (conv * scale * norm_gain[None, :]).astype(jnp.bfloat16)
    mixed = jnp.dot(normed, point_weight, preferred_element_type=jnp.float32)
    encoded = (features.astype(jnp.float32) + jax.nn.gelu(mixed, approximate=False)).astype(
        jnp.bfloat16
    )
    wanted = jnp.concatenate([donor_pos, accept_pos])
    piece = lax.all_gather(encoded, "seq", axis=0, tiled=True)
    inside = (wanted >= 0) & (wanted < piece.shape[0])
    taken = jnp.take(piece, jnp.clip(wanted, 0, piece.shape[0] - 1), axis=0)
    picked = jnp.where(inside[:, None], taken.astype(jnp.float32), jnp.float32(0.0)).astype(
        jnp.bfloat16
    )
    donor_rows = picked[:slots]
    accept_rows = picked[slots:]
    live = jnp.arange(slots, dtype=jnp.int32) < pair_counts[0]
    left = jnp.dot(donor_rows, donor_weight, preferred_element_type=jnp.float32)
    right = jnp.dot(accept_rows, accept_weight, preferred_element_type=jnp.float32)
    junction = jnp.where(live[:, None], jax.nn.silu(left) * right, jnp.float32(0.0)).astype(
        jnp.bfloat16
    )
    return (encoded, junction)


def solution(mesh):
    placed = (
        P(("dp", "seq"), None),
        P(),
        P(),
        P(),
        P(),
        P(),
        P(("dp", "seq")),
        P(("dp", "seq")),
        P(("dp", "seq")),
    )
    return jax.shard_map(
        on_device,
        mesh=mesh,
        in_specs=placed,
        out_specs=(P(("dp", "seq"), None), P(("dp", "seq"), None)),
        check_vma=False,
    )
```

profile of v0, /device:TPU:1, one launch (start us, length us, event | category | flops | bytes accessed | tf_op | source)
XLA Modules:
  0.0 231.2 jit_solution(14900449449986693267)
XLA Ops:
  7.2 0.0 copy-start
  7.2 0.0 all-gather.2.cloned.1.call-start
  7.2 0.9 fusion.25
  8.1 3.9 %collective-permute-start = (bf16[2,1536]{1,0:T(2,128)(2,1)S(1)}, bf16[2,1536]{1,0:T(2,128)(2,1)S(1)}, u32[]{:S(2)}, u32[]{:S(2)}) collective-permute-start(bf16[2,1536]{1,0:T(2,128)(2,1)S(1)} %get-tuple-element.9), channel_id=1, source_target_pairs={{0,1},{1,2},{2,3},{3,4},{4,5},{5,6},{6,7},{7,8},{8,9},{9,10},{10,1... | collective-permute-start | bytes 18440 | tf_op jit(solution)/shard_map/ppermute | solution.py:14
  12.1 1.3 collective-permute-start.1
  13.4 1.1 slice_reduce_fusion.4
  14.5 0.0 collective-permute-done
  14.5 2.0 collective-permute-done.1
  16.5 2.0 maximum_convert_fusion
  18.5 0.0 copy-start.1
  18.5 0.0 slice-start.1
  18.5 0.0 copy-start.5
  18.5 2.4 %multiply_reduce_fusion = (f32[512]{0:T(512)S(1)}, f32[512,1536]{1,0:T(8,128)S(1)}) fusion(f32[516,1536]{1,0:T(8,128)S(1)} %maximum_convert_fusion, f32[1536]{0:T(1024)S(1)} %get-tuple-element.5, f32[1536]{0:T(1024)S(1)} %get-tuple-element.6, f32[1536]{0:T(1024)S(1)} %get-tuple-element.3, f32[1536]{0:T(1024)S(1)} %get-tuple-element.4, ...), kind=kLoop, calls=%fused_computation.29 | loop fusion | flops 8650240 | bytes 18907136 | tf_op jit(solution)/shard_map/reduce_sum | solution.py:37
  21.0 0.0 slice-done
  21.0 0.0 copy-done.1
  21.0 0.0 slice-done.1
  21.0 0.0 copy-done.5
  21.1 0.0 copy-start.2
  21.1 0.0 copy-start.3
  21.1 10.6 %fusion.3 = bf16[512,1536]{1,0:T(8,128)(2,1)} fusion(bf16[512,1536]{1,0:T(8,128)(2,1)S(1)} %copy-done.1, bf16[1536,1536]{1,0:T(8,128)(2,1)S(1)} %bitcast.12, f32[512,1536]{1,0:T(8,128)S(1)} %get-tuple-element.8, f32[1536]{0:T(1024)S(1)} %copy-done.5, f32[512]{0:T(512)S(1)} %add_rsqrt_fusion), kind=kOutput, calls=%fused_computation.5 | convolution fusion | flops 2470969344 | bytes 11018240 | tf_op jit(solution)/shard_map/dot_general | solution.py:39
  31.7 0.0 all-gather.2.cloned.1.call-update
  32.4 0.0 copy-done.2
  32.4 0.0 copy-done.3
  32.4 0.1 fusion.23
  32.5 0.1 compare_and_fusion.1
  32.6 176.3 %all-gather.2.cloned.1.call-done = bf16[8192,1536]{1,0:T(8,128)(2,1)} async-done(((bf16[512,1536]{1,0:T(8,128)(2,1)}), bf16[8192,1536]{1,0:T(8,128)(2,1)}) %all-gather.2.cloned.1.call-update) | async-done | bytes 25165840 | tf_op jit(solution)/shard_map/all_gather | solution.py:44
  208.8 12.6 %gather_fusion = bf16[128,1536]{1,0:T(8,128)(2,1)S(1)} fusion(bf16[8192,1536]{1,0:T(8,128)(2,1)} %all-gather.2.cloned.1.call-done, s32[1024]{0:T(1024)S(1)} %pad_clamp_fusion), kind=kCustom, calls=%fused_computation | custom fusion | bytes 786944 | tf_op jit(solution)/shard_map/jit(_take)/gather | solution.py:46
  221.5 0.0 copy-start.4
  221.5 0.2 select_convert_fusion
  221.7 0.5 fusion.21
  222.2 0.9 copy-done.4
  223.1 1.2 fusion.19
  (6 shorter events, 0.0 us)
Async XLA Ops:
  7.2 214.5 %copy-start = (bf16[1536,768]{1,0:T(8,128)(2,1)S(1)}, bf16[1536,768]{1,0:T(8,128)(2,1)}, u32[]{:S(2)}) copy-start(bf16[1536,768]{1,0:T(8,128)(2,1)} %param.13) | copy-start | bytes 7077892
  7.2 201.6 %all-gather.2.cloned.1.call-start = ((), (), s32[]{:S(2)}) async-start(), calls=%async_computation | async-start | bytes 26738688 | tf_op jit(solution)/shard_map/all_gather | solution.py:44
  8.1 6.3 %collective-permute-start = (bf16[2,1536]{1,0:T(2,128)(2,1)S(1)}, bf16[2,1536]{1,0:T(2,128)(2,1)S(1)}, u32[]{:S(2)}, u32[]{:S(2)}) collective-permute-start(bf16[2,1536]{1,0:T(2,128)(2,1)S(1)} %get-tuple-element.9), channel_id=1, source_target_pairs={{0,1},{1,2},{2,3},{3,4},{4,5},{5,6},{6,7},{7,8},{8,9},{9,10},{10,1... | collective-permute-start | bytes 18440 | tf_op jit(solution)/shard_map/ppermute | solution.py:14
  12.1 4.4 %collective-permute-start.1 = (bf16[2,1536]{1,0:T(2,128)(2,1)S(1)}, bf16[2,1536]{1,0:T(2,128)(2,1)S(1)}, u32[]{:S(2)}, u32[]{:S(2)}) collective-permute-start(bf16[2,1536]{1,0:T(2,128)(2,1)S(1)} %get-tuple-element.10), channel_id=1, source_target_pairs={{1,0},{2,1},{3,2},{4,3},{5,4},{6,5},{7,6},{8,7},{9,8},{10,9},{11,1... | collective-permute-start | bytes 18440 | tf_op jit(solution)/shard_map/ppermute | solution.py:15
  16.5 4.5 %slice-start = ((s8[4718592]{0:T(1024)(128)(4,1)}), s8[4194304]{0:T(1024)(128)(4,1)S(1)}, s32[]{:S(2)}) async-start(s8[4718592]{0:T(1024)(128)(4,1)} %bitcast.11), calls=%async_computation.1 | async-start | bytes 8388608
  18.5 2.5 %copy-start.1 = (bf16[512,1536]{1,0:T(8,128)(2,1)S(1)}, bf16[512,1536]{1,0:T(8,128)(2,1)}, u32[]{:S(2)}) copy-start(bf16[512,1536]{1,0:T(8,128)(2,1)} %param.9) | copy-start | bytes 4718596
  18.5 2.5 %slice-start.1 = ((s8[4718592]{0:T(1024)(128)(4,1)}), s8[524288]{0:T(1024)(128)(4,1)S(1)}, s32[]{:S(2)}) async-start(s8[4718592]{0:T(1024)(128)(4,1)} %bitcast.11), calls=%async_computation.2 | async-start | bytes 1048576
  18.5 2.5 %copy-start.5 = (f32[1536]{0:T(1024)S(1)}, f32[1536]{0:T(1024)}, u32[]{:S(2)}) copy-start(f32[1536]{0:T(1024)} %param.11) | copy-start | bytes 18436
  21.1 11.3 %copy-start.2 = (s32[64]{0:T(128)S(1)}, s32[64]{0:T(128)}, u32[]{:S(2)}) copy-start(s32[64]{0:T(128)} %param.16) | copy-start | bytes 772
  21.1 11.3 %copy-start.3 = (s32[64]{0:T(128)S(1)}, s32[64]{0:T(128)}, u32[]{:S(2)}) copy-start(s32[64]{0:T(128)} %param.15) | copy-start | bytes 772
  221.5 1.7 copy-start.4
Sparse Core Ops, SparseCore 0:
  31.8 176.9 all-gather.1
where the time goes:
time: 231 us
  waiting for transfers between devices  178 us (77%)
  local copies, waits for them, and re-layouts  15.6 us (7%)
  between operations  14.9 us (6%)
  matrix products  12.3 us (5%)
  starting transfers between devices  5.27 us (2%)
  other arithmetic  4.85 us (2%)
    all_gather x1, waiting for transfers between devices, on_device(): piece = lax.all_gather(encoded, 'seq', axis=0, tiled=True)  176 us
    gather x1, local copies, waits for them, and re-layouts, on_device(): taken = jnp.take(piece, jnp.clip(wanted, 0, piece.shape[0] - 1), axis=0)  12.6 us
    dot_general x1, matrix products, on_device(): mixed = jnp.dot(normed, point_weight, preferred_element_type=jnp.float32)  10.6 us
  transfers between devices with their start and end apart: 3, of which 2 were waited for; matrix products, arithmetic and copies ran while one was open for 1% of the time, Pallas kernels for 0%

commit v1 on v0

v1 whole, which is shorter than its diff:
```python
import functools

import jax
import jax.numpy as jnp
from jax import lax
from jax.experimental import pallas as pl
from jax.experimental.pallas import tpu as pltpu
from jax.sharding import PartitionSpec as P

CAP = 16
LANES = 128
WIDE = 256


def gelu(v):
    return 0.5 * v * (1.0 + lax.erf(v * 0.7071067811865476))


def kernel(
    side,
    feat_hbm,
    taps_hbm,
    gain_hbm,
    point_hbm,
    donor_hbm,
    accept_hbm,
    dpos_hbm,
    apos_hbm,
    count_hbm,
    enc_hbm,
    junc_hbm,
    feat,
    taps,
    gain,
    point,
    donor,
    accept,
    dpos,
    apos,
    count,
    padded,
    normed,
    enc,
    junc,
    hot,
    kinds,
    picked,
    edge_out,
    edge_in,
    asks,
    out_rows,
    in_rows,
    load_sem,
    store_sem,
    edge_send,
    edge_recv,
    ask_send,
    ask_recv,
    row_send,
    row_recv,
):
    n = side * side
    rows, channels = feat.shape
    slots = dpos.shape[1]
    width = donor.shape[1]
    lanes = channels // LANES
    me = lax.axis_index("seq")
    my, mx = lax.div(me, side), lax.rem(me, side)

    def ahead(d):
        y = lax.rem(my + lax.div(d, side), side)
        x = lax.rem(mx + lax.rem(d, side), side)
        return y * side + x

    def load(i, source, target):
        return pltpu.make_async_copy(source, target, load_sem.at[i])

    loads = [
        load(0, dpos_hbm, dpos),
        load(1, apos_hbm, apos),
        load(2, count_hbm, count),
        load(3, feat_hbm, feat),
        load(4, taps_hbm, taps),
        load(5, gain_hbm, gain),
        load(6, point_hbm, point),
        load(7, donor_hbm, donor),
        load(8, accept_hbm, accept),
    ]
    for one in loads:
        one.start()

    barrier = pltpu.get_barrier_semaphore()

    @pl.loop(1, n)
    def _(d):
        pl.semaphore_signal(barrier, inc=1, device_id={"seq": ahead(d)})

    loads[0].wait()
    loads[1].wait()
    sub = lax.broadcasted_iota(jnp.int32, (slots, slots), 0)
    lane = lax.broadcasted_iota(jnp.int32, (slots, slots), 1)

    def as_column(row):
        return jnp.sum(
            jnp.where(sub == lane, row.astype(jnp.float32), 0.0), axis=1, keepdims=True
        ).astype(jnp.int32)

    drow, arow = dpos[...], apos[...]
    dcol, acol = as_column(drow), as_column(arow)

    def same(col, row):
        return (col >> 9) == (row >> 9)

    def ones(mask, axis):
        return jnp.sum(jnp.where(mask, 1.0, 0.0), axis=axis, keepdims=True).astype(jnp.int32)

    drank_row = ones(same(dcol, drow) & (sub < lane), 0)
    arank_row = ones(same(acol, arow) & (sub < lane), 0) + ones(same(dcol, arow), 0)
    drank_col = ones(same(dcol, drow) & (lane < sub), 1)
    arank_col = ones(same(acol, arow) & (lane < sub), 1) + ones(same(acol, drow), 1)
    dcode = (dcol >> 9) * CAP + drank_col
    acode = (acol >> 9) * CAP + arank_col
    asks[me, 0:1, :] = (((drow >> 9) * CAP + drank_row) << 9) + (drow & (rows - 1))
    asks[me, 1:2, :] = (((arow >> 9) * CAP + arank_row) << 9) + (arow & (rows - 1))

    loads[3].wait()
    edge_out[0] = feat[0:16, :].astype(jnp.float32)[0:2]
    edge_out[1] = feat[rows - 16 : rows, :].astype(jnp.float32)[14:16]

    pl.semaphore_wait(barrier, n - 1)

    def edge(i, step):
        return pltpu.make_async_remote_copy(
            edge_out.at[i],
            edge_in.at[i],
            edge_send.at[i],
            edge_recv.at[i],
            device_id={"seq": lax.rem(me + step, n)},
        )

    before, after = edge(1, 1), edge(0, n - 1)
    before.start()
    after.start()

    def ask(d):
        return pltpu.make_async_remote_copy(
            asks.at[me], asks.at[me], ask_send.at[d], ask_recv.at[d], device_id={"seq": ahead(d)}
        )

    @pl.loop(1, n)
    def _(d):
        ask(d).start()

    loads[4].wait()
    loads[5].wait()

    @pl.loop(0, rows // 16, unroll=4)
    def _(i):
        at = pl.multiple_of(i * 16, 16)
        padded[pl.ds(at + 8, 16), :] = feat[pl.ds(at, 16), :].astype(jnp.float32)

    def conv_norm(at):
        at = pl.multiple_of(at, 16)
        total = jnp.zeros((16, LANES), jnp.float32)
        parts = []
        for c in range(lanes):
            cols = pl.ds(c * LANES, LANES)
            block = padded[pl.ds(at, 32), cols]
            conv = taps[0:1, cols] * block[6:22]
            for k in range(1, 5):
                conv = conv + taps[k : k + 1, cols] * block[6 + k : 22 + k]
            total = total + conv * conv
            parts.append(conv)
        mean = jnp.sum(total, axis=1, keepdims=True) * (1.0 / channels)
        scale = lax.rsqrt(mean + 1e-6)
        for c in range(lanes):
            cols = pl.ds(c * LANES, LANES)
            normed[pl.ds(at, 16), cols] = (parts[c] * scale * gain[c : c + 1, :]).astype(jnp.bfloat16)

    @pl.loop(1, rows // 16 - 1, unroll=2)
    def _(i):
        conv_norm(i * 16)

    before.wait()
    after.wait()
    zero = jnp.zeros((6, channels), jnp.float32)
    head = jnp.where(me == 0, 0.0, edge_in[1])
    tail = jnp.where(me == n - 1, 0.0, edge_in[0])
    padded[0:8, :] = jnp.concatenate([zero, head], axis=0)
    padded[rows + 8 : rows + 16, :] = jnp.concatenate([tail, zero], axis=0)
    conv_norm(0)
    conv_norm(rows - 16)

    @pl.loop(1, n)
    def _(d):
        ask(d).wait()

    target = me * CAP + lax.broadcasted_iota(jnp.int32, (CAP, slots), 0)
    place = lax.broadcasted_iota(jnp.int32, (CAP, rows), 1)
    for s in range(n):
        d, a = asks[s, 0:1, :], asks[s, 1:2, :]
        found = jnp.where((d >> 9) == target, (d & (rows - 1)).astype(jnp.float32), 0.0)
        found += jnp.where((a >> 9) == target, ((a & (rows - 1)) + rows).astype(jnp.float32), 0.0)
        index = jnp.sum(found, axis=1, keepdims=True).astype(jnp.int32)
        hot[s * CAP : (s + 1) * CAP, :] = jnp.where(
            (index & (rows - 1)) == place, 1.0, 0.0
        ).astype(jnp.bfloat16)
        kinds[s * CAP : (s + 1) * CAP, :] = jnp.broadcast_to(index, (CAP, LANES))

    loads[6].wait()
    stores = []
    for c in range(channels // WIDE):
        cols = slice(c * WIDE, (c + 1) * WIDE)
        mixed = jnp.dot(normed[...], point[:, cols], preferred_element_type=jnp.float32)
        enc[:, cols] = (feat[:, cols].astype(jnp.float32) + gelu(mixed)).astype(jnp.bfloat16)
        picked[:, cols] = jnp.dot(
            hot[...], enc[:, cols], preferred_element_type=jnp.float32
        ).astype(jnp.bfloat16)
    store = pltpu.make_async_copy(enc, enc_hbm, store_sem.at[0])
    store.start()

    loads[7].wait()
    loads[8].wait()
    is_accept = jnp.concatenate([kinds[...] >= rows] * (WIDE // LANES), axis=1)
    for c in range(width // WIDE):
        cols = slice(c * WIDE, (c + 1) * WIDE)
        left = jnp.dot(picked[...], donor[:, cols], preferred_element_type=jnp.float32)
        right = jnp.dot(picked[...], accept[:, cols], preferred_element_type=jnp.float32)
        out_rows[:, :, cols] = (
            jnp.where(is_accept, right, left).astype(jnp.bfloat16).reshape(n, CAP, WIDE)
        )

    def send(d):
        return pltpu.make_async_remote_copy(
            out_rows.at[ahead(d)],
            in_rows.at[me],
            row_send.at[d],
            row_recv.at[d],
            device_id={"seq": ahead(d)},
        )

    @pl.loop(1, n)
    def _(d):
        send(d).start()

    in_rows[me] = out_rows[me]
    loads[2].wait()
    live = lax.broadcasted_iota(jnp.int32, (slots, width), 0) < count[0]
    spot = lax.broadcasted_iota(jnp.int32, (slots, n * CAP), 1)
    dhot = jnp.where(spot == dcode, 1.0, 0.0).astype(jnp.bfloat16)
    ahot = jnp.where(spot == acode, 1.0, 0.0).astype(jnp.bfloat16)

    @pl.loop(1, n)
    def _(d):
        send(d).wait()

    got = in_rows[...].reshape(n * CAP, width)
    left = jnp.dot(dhot, got, preferred_element_type=jnp.float32)
    right = jnp.dot(ahot, got, preferred_element_type=jnp.float32)
    gated = left / (1.0 + jnp.exp(-left)) * right
    junc[...] = jnp.where(live, gated, 0.0).astype(jnp.bfloat16)
    last = pltpu.make_async_copy(junc, junc_hbm, store_sem.at[1])
    last.start()
    last.wait()
    store.wait()


def on_device(side, features, taps, gain, point, donor, accept, dpos, apos, counts):
    rows, channels = features.shape
    slots = dpos.shape[0]
    width = donor.shape[1]
    n = side * side
    f32, bf16, i32 = jnp.float32, jnp.bfloat16, jnp.int32
    dma = pltpu.SemaphoreType.DMA
    return pl.pallas_call(
        functools.partial(kernel, side),
        out_shape=(
            jax.ShapeDtypeStruct((rows, channels), bf16),
            jax.ShapeDtypeStruct((slots, width), bf16),
        ),
        in_specs=[pl.BlockSpec(memory_space=pltpu.HBM)] * 9,
        out_specs=[pl.BlockSpec(memory_space=pl.ANY)] * 2,
        scratch_shapes=[
            pltpu.VMEM((rows, channels), bf16),
            pltpu.VMEM(taps.shape, f32),
            pltpu.VMEM((channels // LANES, LANES), f32),
            pltpu.VMEM((channels, channels), bf16),
            pltpu.VMEM((channels, width), bf16),
            pltpu.VMEM((channels, width), bf16),
            pltpu.VMEM((1, slots), i32),
            pltpu.VMEM((1, slots), i32),
            pltpu.SMEM((1,), i32),
            pltpu.VMEM((rows + 16, channels), f32),
            pltpu.VMEM((rows, channels), bf16),
            pltpu.VMEM((rows, channels), bf16),
            pltpu.VMEM((slots, width), bf16),
            pltpu.VMEM((n * CAP, rows), bf16),
            pltpu.VMEM((n * CAP, LANES), i32),
            pltpu.VMEM((n * CAP, channels), bf16),
            pltpu.VMEM((2, 2, channels), f32),
            pltpu.VMEM((2, 2, channels), f32),
            pltpu.VMEM((n, 2, slots), i32),
            pltpu.VMEM((n, CAP, width), bf16),
            pltpu.VMEM((n, CAP, width), bf16),
            dma((9,)),
            dma((2,)),
            dma((2,)),
            dma((2,)),
            dma((n,)),
            dma((n,)),
            dma((n,)),
            dma((n,)),
        ],
        compiler_params=pltpu.CompilerParams(
            collective_id=0, has_side_effects=True, vmem_limit_bytes=56 * 1024 * 1024
        ),
        cost_estimate=pl.CostEstimate(
            flops=2 * rows * channels * channels,
            bytes_accessed=12 * 1024 * 1024,
            transcendentals=rows * channels,
        ),
    )(
        features,
        taps,
        gain.reshape(channels // LANES, LANES),
        point,
        donor,
        accept,
        dpos.reshape(1, slots),
        apos.reshape(1, slots),
        counts,
    )


def solution(mesh):
    side = 4
    placed = (
        P(("dp", "seq"), None),
        P(),
        P(),
        P(),
        P(),
        P(),
        P(("dp", "seq")),
        P(("dp", "seq")),
        P(("dp", "seq")),
    )
    return jax.shard_map(
        functools.partial(on_device, side),
        mesh=mesh,
        in_specs=placed,
        out_specs=(P(("dp", "seq"), None), P(("dp", "seq"), None)),
        check_vma=False,
    )
```

time: 231 us -> 34.2 us (0.15)
  the two profiles are of different devices: /device:TPU:1 before, /device:TPU:8 now
where the time goes in v1:
time: 34.2 us; the launch traced here: 34.1 us
  Pallas kernels  29.4 us (86%)
  local copies, waits for them, and re-layouts  3.33 us (10%)
  between operations  1.3 us (4%)
    pallas_call x1, Pallas kernels, on_device(): pl.pallas_call(functools.partial(kernel, side), out_shape=(jax.ShapeDtype...  29.4 us
    unnamed x4, local copies, waits for them, and re-layouts  3.33 us

profile of v1, /device:TPU:8, one launch (start us, length us, event | category | flops | bytes accessed | tf_op | source)
XLA Modules:
  0.0 34.1 jit_solution(17291762224541314783)
XLA Ops:
  1.3 29.4 %shard_map.104 = (bf16[512,1536]{1,0:T(8,128)(2,1)}, bf16[64,768]{1,0:T(8,128)(2,1)}) custom-call(bf16[512,1536]{1,0:T(8,128)(2,1)} %feat_hbm.1, f32[5,1536]{1,0:T(8,128)} %taps_hbm.1, f32[12,128]{1,0:T(8,128)} %bitcast.3, bf16[1536,1536]{1,0:T(8,128)(2,1)} %point_hbm.1, bf16[1536,768]{1,0:T(8,128)(2,1)} %donor_hbm.1, bf16[1536,768]{1,0:T(8,128)(2,1)} %accept_hbm.1, ...), custom_call_target="tpu_custom_call" | custom-call | flops 2415919104 | bytes 12582912 | tf_op jit(solution)/shard_map/pallas_call | solution.py:275
  30.7 0.0 copy-start
  30.7 2.7 %copy.14 = bf16[512,1536]{1,0:T(8,128)(2,1)} copy(bf16[512,1536]{1,0:T(8,128)(2,1)} %get-tuple-element.4) | data formatting | bytes 3145728
  33.4 0.0 copy-done
  33.4 0.6 %copy.15 = bf16[64,768]{1,0:T(8,128)(2,1)} copy(bf16[64,768]{1,0:T(8,128)(2,1)S(1)} %copy-done) | data formatting | bytes 196608
Async XLA Ops:
  30.7 2.7 %copy-start = (bf16[64,768]{1,0:T(8,128)(2,1)S(1)}, bf16[64,768]{1,0:T(8,128)(2,1)}, u32[]{:S(2)}) copy-start(bf16[64,768]{1,0:T(8,128)(2,1)} %get-tuple-element.5) | copy-start | bytes 294916

commit v2 on v1

v2 whole, which is shorter than its diff:
```python
import functools

import jax
import jax.numpy as jnp
from jax import lax
from jax.experimental import pallas as pl
from jax.experimental.pallas import tpu as pltpu
from jax.sharding import PartitionSpec as P

CAP = 16
LANES = 128
WIDE = 256


def gelu(v):
    return 0.5 * v * (1.0 + lax.erf(v * 0.7071067811865476))


def kernel(
    side,
    feat_hbm,
    taps_hbm,
    gain_hbm,
    point_hbm,
    donor_hbm,
    accept_hbm,
    dpos_hbm,
    apos_hbm,
    count,
    enc,
    in_rows,
    dhot,
    ahot,
    feat,
    taps,
    gain,
    point,
    donor,
    accept,
    dpos,
    apos,
    padded,
    normed,
    hot,
    kinds,
    picked,
    edge_out,
    edge_in,
    asks,
    out_rows,
    load_sem,
    edge_send,
    edge_recv,
    ask_send,
    ask_recv,
    row_send,
    row_recv,
):
    n = side * side
    rows, channels = feat.shape
    slots = dpos.shape[1]
    width = donor.shape[1]
    lanes = channels // LANES
    me = lax.axis_index("seq")
    my, mx = lax.div(me, side), lax.rem(me, side)

    def ahead(d):
        y = lax.rem(my + lax.div(d, side), side)
        x = lax.rem(mx + lax.rem(d, side), side)
        return y * side + x

    def load(i, source, target):
        return pltpu.make_async_copy(source, target, load_sem.at[i])

    loads = [
        load(0, dpos_hbm, dpos),
        load(1, apos_hbm, apos),
        load(2, feat_hbm, feat),
        load(3, taps_hbm, taps),
        load(4, gain_hbm, gain),
        load(5, point_hbm, point),
        load(6, donor_hbm, donor),
        load(7, accept_hbm, accept),
    ]
    for one in loads:
        one.start()

    barrier = pltpu.get_barrier_semaphore()

    @pl.loop(1, n)
    def _(d):
        pl.semaphore_signal(barrier, inc=1, device_id={"seq": ahead(d)})

    loads[0].wait()
    loads[1].wait()
    sub = lax.broadcasted_iota(jnp.int32, (slots, slots), 0)
    lane = lax.broadcasted_iota(jnp.int32, (slots, slots), 1)

    def as_column(row):
        return jnp.sum(
            jnp.where(sub == lane, row.astype(jnp.float32), 0.0), axis=1, keepdims=True
        ).astype(jnp.int32)

    drow, arow = dpos[...], apos[...]
    dcol, acol = as_column(drow), as_column(arow)

    def same(col, row):
        return (col >> 9) == (row >> 9)

    def ones(mask, axis):
        return jnp.sum(jnp.where(mask, 1.0, 0.0), axis=axis, keepdims=True).astype(jnp.int32)

    drank_row = ones(same(dcol, drow) & (sub < lane), 0)
    arank_row = ones(same(acol, arow) & (sub < lane), 0) + ones(same(dcol, arow), 0)
    drank_col = ones(same(dcol, drow) & (lane < sub), 1)
    arank_col = ones(same(acol, arow) & (lane < sub), 1) + ones(same(acol, drow), 1)
    dcode = (dcol >> 9) * CAP + drank_col
    acode = (acol >> 9) * CAP + arank_col
    asks[me, 0:1, :] = (((drow >> 9) * CAP + drank_row) << 9) + (drow & (rows - 1))
    asks[me, 1:2, :] = (((arow >> 9) * CAP + arank_row) << 9) + (arow & (rows - 1))
    spot = lax.broadcasted_iota(jnp.int32, (slots, n * CAP), 1)
    slot = lax.broadcasted_iota(jnp.int32, (slots, n * CAP), 0)
    live = slot < count[0]
    dhot[...] = jnp.where((spot == dcode) & live, 1.0, 0.0).astype(jnp.bfloat16)
    ahot[...] = jnp.where(spot == acode, 1.0, 0.0).astype(jnp.bfloat16)

    loads[2].wait()
    loads[3].wait()
    loads[4].wait()

    def widen(at, count):
        for c in range(lanes):
            padded[c, at + 8 : at + 8 + count, :] = feat[
                at : at + count, c * LANES : (c + 1) * LANES
            ].astype(jnp.float32)

    def conv_norm(at, count):
        total = jnp.zeros((count, LANES), jnp.float32)
        parts = []
        for c in range(lanes):
            cols = slice(c * LANES, (c + 1) * LANES)
            conv = taps[0:1, cols] * padded[c, at + 6 : at + 6 + count, :]
            for k in range(1, 5):
                conv = conv + taps[k : k + 1, cols] * padded[c, at + 6 + k : at + 6 + k + count, :]
            total = total + conv * conv
            parts.append(conv)
        mean = jnp.sum(total, axis=1, keepdims=True) * (1.0 / channels)
        scale = lax.rsqrt(mean + 1e-6)
        for c in range(lanes):
            cols = slice(c * LANES, (c + 1) * LANES)
            normed[at : at + count, cols] = (parts[c] * scale * gain[c : c + 1, :]).astype(
                jnp.bfloat16
            )

    widen(0, 32)
    for at in range(16, rows - 16, 32):
        widen(at + 16, min(32, rows - at - 16))
        conv_norm(at, min(32, rows - 16 - at))
    for c in range(lanes):
        edge_out[0, 2 * c : 2 * c + 2, :] = padded[c, 8:10, :]
        edge_out[1, 2 * c : 2 * c + 2, :] = padded[c, rows + 6 : rows + 8, :]

    pl.semaphore_wait(barrier, n - 1)

    def edge(i, step):
        return pltpu.make_async_remote_copy(
            edge_out.at[i],
            edge_in.at[i],
            edge_send.at[i],
            edge_recv.at[i],
            device_id={"seq": lax.rem(me + step, n)},
        )

    def ask(d):
        return pltpu.make_async_remote_copy(
            asks.at[me], asks.at[me], ask_send.at[d], ask_recv.at[d], device_id={"seq": ahead(d)}
        )

    before, after = edge(1, 1), edge(0, n - 1)
    before.start()
    after.start()

    @pl.loop(1, n)
    def _(d):
        ask(d).start()

    loads[5].wait()

    def encode(spans):
        for c in range(channels // WIDE):
            cols = slice(c * WIDE, (c + 1) * WIDE)
            source = jnp.concatenate([normed[a:b, :] for a, b in spans], axis=0)
            mixed = jnp.dot(source, point[:, cols], preferred_element_type=jnp.float32)
            at = 0
            for a, b in spans:
                part = mixed[at : at + b - a]
                at += b - a
                enc[a:b, cols] = (feat[a:b, cols].astype(jnp.float32) + gelu(part)).astype(
                    jnp.bfloat16
                )

    encode([(16, rows - 16)])
    loads[6].wait()
    loads[7].wait()
    before.wait()
    after.wait()

    @pl.loop(1, n)
    def _(d):
        ask(d).wait()

    for c in range(lanes):
        padded[c, 6:8, :] = jnp.where(me == 0, 0.0, edge_in[1, 2 * c : 2 * c + 2, :])
        padded[c, rows + 8 : rows + 10, :] = jnp.where(
            me == n - 1, 0.0, edge_in[0, 2 * c : 2 * c + 2, :]
        )
    conv_norm(0, 16)
    conv_norm(rows - 16, 16)
    encode([(0, 16), (rows - 16, rows)])

    target = me * CAP + lax.broadcasted_iota(jnp.int32, (CAP, slots), 0)
    place = lax.broadcasted_iota(jnp.int32, (CAP, rows), 1)
    for s in range(n):
        d, a = asks[s, 0:1, :], asks[s, 1:2, :]
        found = jnp.where((d >> 9) == target, (d & (rows - 1)).astype(jnp.float32), 0.0)
        found += jnp.where((a >> 9) == target, ((a & (rows - 1)) + rows).astype(jnp.float32), 0.0)
        index = jnp.sum(found, axis=1, keepdims=True).astype(jnp.int32)
        hot[s * CAP : (s + 1) * CAP, :] = jnp.where(
            (index & (rows - 1)) == place, 1.0, 0.0
        ).astype(jnp.bfloat16)
        kinds[s * CAP : (s + 1) * CAP, :] = jnp.broadcast_to(index, (CAP, LANES))

    for c in range(channels // WIDE):
        cols = slice(c * WIDE, (c + 1) * WIDE)
        picked[:, cols] = jnp.dot(
            hot[...], enc[:, cols], preferred_element_type=jnp.float32
        ).astype(jnp.bfloat16)

    def send(c, d):
        return pltpu.make_async_remote_copy(
            out_rows.at[c, ahead(d)],
            in_rows.at[c, me],
            row_send.at[c, d],
            row_recv.at[c, d],
            device_id={"seq": ahead(d)},
        )

    is_accept = jnp.concatenate([kinds[...] >= rows] * (WIDE // LANES), axis=1)
    for c in range(width // WIDE):
        cols = slice(c * WIDE, (c + 1) * WIDE)
        left = jnp.dot(picked[...], donor[:, cols], preferred_element_type=jnp.float32)
        right = jnp.dot(picked[...], accept[:, cols], preferred_element_type=jnp.float32)
        out_rows[c] = jnp.where(is_accept, right, left).astype(jnp.bfloat16).reshape(n, CAP, WIDE)

        @pl.loop(1, n)
        def _(d):
            send(c, d).start()

    for c in range(width // WIDE):
        in_rows[c, me] = out_rows[c, me]

        @pl.loop(1, n)
        def _(d):
            send(c, d).wait()


def finish(enc, in_rows, dhot, ahot, enc_hbm, junc_hbm, junc, sem):
    store = pltpu.make_async_copy(enc, enc_hbm, sem.at[0])
    store.start()
    blocks, n, cap, wide = in_rows.shape
    for c in range(blocks):
        got = in_rows[c].reshape(n * cap, wide)
        left = jnp.dot(dhot[...], got, preferred_element_type=jnp.float32)
        right = jnp.dot(ahot[...], got, preferred_element_type=jnp.float32)
        junc[:, c * wide : (c + 1) * wide] = (left / (1.0 + jnp.exp(-left)) * right).astype(
            jnp.bfloat16
        )
    last = pltpu.make_async_copy(junc, junc_hbm, sem.at[1])
    last.start()
    last.wait()
    store.wait()


def on_device(side, features, taps, gain, point, donor, accept, dpos, apos, counts):
    rows, channels = features.shape
    slots = dpos.shape[0]
    width = donor.shape[1]
    n = side * side
    blocks = width // WIDE
    f32, bf16, i32 = jnp.float32, jnp.bfloat16, jnp.int32
    dma = pltpu.SemaphoreType.DMA
    held = pl.pallas_call(
        functools.partial(kernel, side),
        out_shape=(
            pltpu.VMEM((rows, channels), bf16),
            pltpu.VMEM((blocks, n, CAP, WIDE), bf16),
            pltpu.VMEM((slots, n * CAP), bf16),
            pltpu.VMEM((slots, n * CAP), bf16),
        ),
        in_specs=[pl.BlockSpec(memory_space=pltpu.HBM)] * 8
        + [pl.BlockSpec(memory_space=pltpu.SMEM)],
        out_specs=[pl.BlockSpec(memory_space=pltpu.VMEM)] * 4,
        scratch_shapes=[
            pltpu.VMEM((rows, channels), bf16),
            pltpu.VMEM(taps.shape, f32),
            pltpu.VMEM((channels // LANES, LANES), f32),
            pltpu.VMEM((channels, channels), bf16),
            pltpu.VMEM((channels, width), bf16),
            pltpu.VMEM((channels, width), bf16),
            pltpu.VMEM((1, slots), i32),
            pltpu.VMEM((1, slots), i32),
            pltpu.VMEM((channels // LANES, rows + 16, LANES), f32),
            pltpu.VMEM((rows, channels), bf16),
            pltpu.VMEM((n * CAP, rows), bf16),
            pltpu.VMEM((n * CAP, LANES), i32),
            pltpu.VMEM((n * CAP, channels), bf16),
            pltpu.VMEM((2, 2 * channels // LANES, LANES), f32),
            pltpu.VMEM((2, 2 * channels // LANES, LANES), f32),
            pltpu.VMEM((n, 2, slots), i32),
            pltpu.VMEM((blocks, n, CAP, WIDE), bf16),
            dma((8,)),
            dma((2,)),
            dma((2,)),
            dma((n,)),
            dma((n,)),
            dma((blocks, n)),
            dma((blocks, n)),
        ],
        compiler_params=pltpu.CompilerParams(
            collective_id=0, has_side_effects=True, vmem_limit_bytes=40 * 1024 * 1024
        ),
    )(
        *(
            pltpu.with_memory_space_constraint(v, pltpu.HBM)
            for v in (
                features,
                taps,
                gain.reshape(channels // LANES, LANES),
                point,
                donor,
                accept,
                dpos.reshape(1, slots),
                apos.reshape(1, slots),
            )
        ),
        counts,
    )
    return pl.pallas_call(
        finish,
        out_shape=(
            jax.ShapeDtypeStruct((rows, channels), bf16),
            jax.ShapeDtypeStruct((slots, width), bf16),
        ),
        in_specs=[pl.BlockSpec(memory_space=pltpu.VMEM)] * 4,
        out_specs=[pl.BlockSpec(memory_space=pltpu.HBM)] * 2,
        scratch_shapes=[pltpu.VMEM((slots, width), bf16), dma((2,))],
        compiler_params=pltpu.CompilerParams(vmem_limit_bytes=8 * 1024 * 1024),
    )(*held)


def solution(mesh):
    side = 4
    placed = (
        P(("dp", "seq"), None),
        P(),
        P(),
        P(),
        P(),
        P(),
        P(("dp", "seq")),
        P(("dp", "seq")),
        P(("dp", "seq")),
    )
    return jax.shard_map(
        functools.partial(on_device, side),
        mesh=mesh,
        in_specs=placed,
        out_specs=(P(("dp", "seq"), None), P(("dp", "seq"), None)),
        check_vma=False,
    )
```

time: 34.2 us -> 25.6 us (0.75)
  Pallas kernels: 29.4 us -> 24.1 us
  local copies, waits for them, and re-layouts: 3.33 us -> 0 us
    pallas_call x1 -> x2, Pallas kernels: 29.4 us -> 24.1 us  [the longest x1 22.9 us: on_device(): pl.pallas_call(functools.partial(kernel, side), out_shape=(pltpu.VMEM((ro...]
    unnamed x4 -> x0, local copies, waits for them, and re-layouts: 3.33 us -> none
where the time goes in v2:
time: 25.6 us; the launch traced here: 25.4 us
  Pallas kernels  24.1 us (94%)
  between operations  1.29 us (5%)
    pallas_call x1, Pallas kernels, on_device(): pl.pallas_call(functools.partial(kernel, side), out_shape=(pltpu.VMEM((ro...  22.9 us
    pallas_call x1, Pallas kernels, on_device(): pl.pallas_call(finish, out_shape=(jax.ShapeDtypeStruct((rows, channels),...  1.19 us

profile of v2, /device:TPU:8, one launch (start us, length us, event | category | flops | bytes accessed | tf_op | source)
XLA Modules:
  0.0 25.4 jit_solution(4401203526063655075)
XLA Ops:
  1.3 22.9 %shard_map.104 = (bf16[512,1536]{1,0:T(8,128)(2,1)S(1)}, bf16[3,16,16,256]{3,2,1,0:T(8,128)(2,1)S(1)}, bf16[64,256]{1,0:T(8,128)(2,1)S(1)}, bf16[64,256]{1,0:T(8,128)(2,1)S(1)}) custom-call(bf16[512,1536]{1,0:T(8,128)(2,1)} %feat_hbm.1, f32[5,1536]{1,0:T(8,128)} %taps_hbm.1, f32[12,128]{1,0:T(8,128)} %bitcast.3, bf16[1536,1536]{1,0:T(8,128)(2,1)} %point_hbm.1, ...), custom_call_target="tpu_custom_call" | custom-call | tf_op jit(solution)/shard_map/pallas_call | solution.py:292
  24.2 1.2 %shard_map.105 = (bf16[512,1536]{1,0:T(8,128)(2,1)}, bf16[64,768]{1,0:T(8,128)(2,1)}) custom-call(bf16[512,1536]{1,0:T(8,128)(2,1)S(1)} %get-tuple-element.6.enc, bf16[3,16,16,256]{3,2,1,0:T(8,128)(2,1)S(1)} %get-tuple-element.7.in_rows, bf16[64,256]{1,0:T(8,128)(2,1)S(1)} %get-tuple-element.8.dhot, bf16[64,256]{1,0:T(8,128)(2,1)S(1)} %get-tuple-element.9.ahot), custom_call_target="tpu_custom_call" | custom-call | tf_op jit(solution)/shard_map/pallas_call | solution.py:348

commit v3 on v2

--- a/solution.py
+++ b/solution.py
@@ -75,21 +75,23 @@
     loads = [
         load(0, dpos_hbm, dpos),
         load(1, apos_hbm, apos),
-        load(2, feat_hbm, feat),
-        load(3, taps_hbm, taps),
-        load(4, gain_hbm, gain),
-        load(5, point_hbm, point),
-        load(6, donor_hbm, donor),
-        load(7, accept_hbm, accept),
+        load(2, feat_hbm.at[0:16], feat.at[0:16]),
+        load(3, feat_hbm.at[rows - 16 : rows], feat.at[rows - 16 : rows]),
+        load(4, taps_hbm, taps),
+        load(5, gain_hbm, gain),
+        load(6, feat_hbm.at[16 : rows - 16], feat.at[16 : rows - 16]),
+        load(7, point_hbm, point),
+        load(8, donor_hbm, donor),
+        load(9, accept_hbm, accept),
     ]
-    for one in loads:
-        one.start()
-
     barrier = pltpu.get_barrier_semaphore()
 
     @pl.loop(1, n)
     def _(d):
         pl.semaphore_signal(barrier, inc=1, device_id={"seq": ahead(d)})
+
+    for one in loads:
+        one.start()
 
     loads[0].wait()
     loads[1].wait()
@@ -123,10 +125,6 @@
     live = slot < count[0]
     dhot[...] = jnp.where((spot == dcode) & live, 1.0, 0.0).astype(jnp.bfloat16)
     ahot[...] = jnp.where(spot == acode, 1.0, 0.0).astype(jnp.bfloat16)
-
-    loads[2].wait()
-    loads[3].wait()
-    loads[4].wait()
 
     def widen(at, count):
         for c in range(lanes):
@@ -152,13 +150,22 @@
                 jnp.bfloat16
             )
 
-    widen(0, 32)
-    for at in range(16, rows - 16, 32):
-        widen(at + 16, min(32, rows - at - 16))
-        conv_norm(at, min(32, rows - 16 - at))
+    loads[2].wait()
+    loads[3].wait()
+    widen(0, 16)
+    widen(rows - 16, 16)
     for c in range(lanes):
         edge_out[0, 2 * c : 2 * c + 2, :] = padded[c, 8:10, :]
         edge_out[1, 2 * c : 2 * c + 2, :] = padded[c, rows + 6 : rows + 8, :]
+
+    loads[4].wait()
+    loads[5].wait()
+    loads[6].wait()
+    widen(16, 32)
+    for at in range(16, 240, 32):
+        if at + 32 < rows - 16:
+            widen(at + 32, min(32, rows - 16 - at - 32))
+        conv_norm(at, min(32, rows - 16 - at))
 
     pl.semaphore_wait(barrier, n - 1)
 
@@ -184,7 +191,10 @@
     def _(d):
         ask(d).start()
 
-    loads[5].wait()
+    for at in range(240, rows - 16, 32):
+        if at + 32 < rows - 16:
+            widen(at + 32, min(32, rows - 16 - at - 32))
+        conv_norm(at, min(32, rows - 16 - at))
 
     def encode(spans):
         for c in range(channels // WIDE):
@@ -199,15 +209,13 @@
                     jnp.bfloat16
                 )
 
-    encode([(16, rows - 16)])
-    loads[6].wait()
     loads[7].wait()
+    half = rows // 2
+    encode([(16, 16 + half)])
+    loads[8].wait()
+    loads[9].wait()
     before.wait()
     after.wait()
-
-    @pl.loop(1, n)
-    def _(d):
-        ask(d).wait()
 
     for c in range(lanes):
         padded[c, 6:8, :] = jnp.where(me == 0, 0.0, edge_in[1, 2 * c : 2 * c + 2, :])
@@ -216,7 +224,12 @@
         )
     conv_norm(0, 16)
     conv_norm(rows - 16, 16)
-    encode([(0, 16), (rows - 16, rows)])
+    encode([(0, 16), (16 + half, rows)])
+
+    @pl.loop(1, n)
+    def _(d):
+        ask(d).wait()
+
 
     target = me * CAP + lax.broadcasted_iota(jnp.int32, (CAP, slots), 0)
     place = lax.broadcasted_iota(jnp.int32, (CAP, rows), 1)
@@ -245,15 +258,18 @@
             device_id={"seq": ahead(d)},
         )
 
+    def hops(d):
+        y, x = divmod(d, side)
+        return min(y, side - y) + min(x, side - x)
+
+    order = sorted(range(1, n), key=lambda d: -hops(d))
     is_accept = jnp.concatenate([kinds[...] >= rows] * (WIDE // LANES), axis=1)
     for c in range(width // WIDE):
         cols = slice(c * WIDE, (c + 1) * WIDE)
         left = jnp.dot(picked[...], donor[:, cols], preferred_element_type=jnp.float32)
         right = jnp.dot(picked[...], accept[:, cols], preferred_element_type=jnp.float32)
         out_rows[c] = jnp.where(is_accept, right, left).astype(jnp.bfloat16).reshape(n, CAP, WIDE)
-
-        @pl.loop(1, n)
-        def _(d):
+        for d in order:
             send(c, d).start()
 
     for c in range(width // WIDE):
@@ -318,7 +334,7 @@
             pltpu.VMEM((2, 2 * channels // LANES, LANES), f32),
             pltpu.VMEM((n, 2, slots), i32),
             pltpu.VMEM((blocks, n, CAP, WIDE), bf16),
-            dma((8,)),
+            dma((10,)),
             dma((2,)),
             dma((2,)),
             dma((n,)),

time: 25.6 us -> 24.9 us (0.973)
  the two profiles are of different devices: /device:TPU:8 before, /device:TPU:2 now
where the time goes in v3:
time: 24.9 us; the launch traced here: 24.8 us
  Pallas kernels  23.5 us (94%)
  between operations  1.29 us (5%)
    pallas_call x1, Pallas kernels, on_device(): pl.pallas_call(functools.partial(kernel, side), out_shape=(pltpu.VMEM((ro...  22.3 us
    pallas_call x1, Pallas kernels, on_device(): pl.pallas_call(finish, out_shape=(jax.ShapeDtypeStruct((rows, channels),...  1.19 us

profile of v3, /device:TPU:2, one launch (start us, length us, event | category | flops | bytes accessed | tf_op | source)
XLA Modules:
  0.0 24.8 jit_solution(16970021610948286848)
XLA Ops:
  1.3 22.3 %shard_map.104 = (bf16[512,1536]{1,0:T(8,128)(2,1)S(1)}, bf16[3,16,16,256]{3,2,1,0:T(8,128)(2,1)S(1)}, bf16[64,256]{1,0:T(8,128)(2,1)S(1)}, bf16[64,256]{1,0:T(8,128)(2,1)S(1)}) custom-call(bf16[512,1536]{1,0:T(8,128)(2,1)} %feat_hbm.1, f32[5,1536]{1,0:T(8,128)} %taps_hbm.1, f32[12,128]{1,0:T(8,128)} %bitcast.3, bf16[1536,1536]{1,0:T(8,128)(2,1)} %point_hbm.1, ...), custom_call_target="tpu_custom_call" | custom-call | tf_op jit(solution)/shard_map/pallas_call | solution.py:308
  23.6 1.2 %shard_map.105 = (bf16[512,1536]{1,0:T(8,128)(2,1)}, bf16[64,768]{1,0:T(8,128)(2,1)}) custom-call(bf16[512,1536]{1,0:T(8,128)(2,1)S(1)} %get-tuple-element.6.enc, bf16[3,16,16,256]{3,2,1,0:T(8,128)(2,1)S(1)} %get-tuple-element.7.in_rows, bf16[64,256]{1,0:T(8,128)(2,1)S(1)} %get-tuple-element.8.dhot, bf16[64,256]{1,0:T(8,128)(2,1)S(1)} %get-tuple-element.9.ahot), custom_call_target="tpu_custom_call" | custom-call | tf_op jit(solution)/shard_map/pallas_call | solution.py:364

commit v4 on v3

--- a/solution.py
+++ b/solution.py
@@ -64,10 +64,9 @@
     me = lax.axis_index("seq")
     my, mx = lax.div(me, side), lax.rem(me, side)
 
-    def ahead(d):
-        y = lax.rem(my + lax.div(d, side), side)
-        x = lax.rem(mx + lax.rem(d, side), side)
-        return y * side + x
+    ys = [lax.rem(my + d, side) * side for d in range(side)]
+    xs = [lax.rem(mx + d, side) for d in range(side)]
+    peers = [ys[d // side] + xs[d % side] for d in range(n)]
 
     def load(i, source, target):
         return pltpu.make_async_copy(source, target, load_sem.at[i])
@@ -86,9 +85,8 @@
     ]
     barrier = pltpu.get_barrier_semaphore()
 
-    @pl.loop(1, n)
-    def _(d):
-        pl.semaphore_signal(barrier, inc=1, device_id={"seq": ahead(d)})
+    for d in range(1, n):
+        pl.semaphore_signal(barrier, inc=1, device_id={"seq": peers[d]})
 
     for one in loads:
         one.start()
@@ -180,15 +178,14 @@
 
     def ask(d):
         return pltpu.make_async_remote_copy(
-            asks.at[me], asks.at[me], ask_send.at[d], ask_recv.at[d], device_id={"seq": ahead(d)}
+            asks.at[me], asks.at[me], ask_send.at[d], ask_recv.at[d], device_id={"seq": peers[d]}
         )
 
     before, after = edge(1, 1), edge(0, n - 1)
     before.start()
     after.start()
 
-    @pl.loop(1, n)
-    def _(d):
+    for d in range(1, n):
         ask(d).start()
 
     for at in range(240, rows - 16, 32):
@@ -210,7 +207,7 @@
                 )
 
     loads[7].wait()
-    half = rows // 2
+    half = 384
     encode([(16, 16 + half)])
     loads[8].wait()
     loads[9].wait()
@@ -226,8 +223,7 @@
     conv_norm(rows - 16, 16)
     encode([(0, 16), (16 + half, rows)])
 
-    @pl.loop(1, n)
-    def _(d):
+    for d in range(1, n):
         ask(d).wait()
 
 
@@ -251,11 +247,11 @@
 
     def send(c, d):
         return pltpu.make_async_remote_copy(
-            out_rows.at[c, ahead(d)],
+            out_rows.at[c, peers[d]],
             in_rows.at[c, me],
             row_send.at[c, d],
             row_recv.at[c, d],
-            device_id={"seq": ahead(d)},
+            device_id={"seq": peers[d]},
         )
 
     def hops(d):
@@ -274,9 +270,7 @@
 
     for c in range(width // WIDE):
         in_rows[c, me] = out_rows[c, me]
-
-        @pl.loop(1, n)
-        def _(d):
+        for d in order:
             send(c, d).wait()
 
 

time: 24.9 us -> 24.1 us (0.968)
  Pallas kernels: 23.5 us -> 22.6 us
    pallas_call x1, Pallas kernels: 22.3 us -> 21.5 us  [on_device(): pl.pallas_call(functools.partial(kernel, side), out_shape=(pltpu.VMEM((ro...]
where the time goes in v4:
time: 24.1 us; the launch traced here: 23.9 us
  Pallas kernels  22.6 us (94%)
  between operations  1.29 us (5%)
    pallas_call x1, Pallas kernels, on_device(): pl.pallas_call(functools.partial(kernel, side), out_shape=(pltpu.VMEM((ro...  21.5 us
    pallas_call x1, Pallas kernels, on_device(): pl.pallas_call(finish, out_shape=(jax.ShapeDtypeStruct((rows, channels),...  1.19 us

profile of v4, /device:TPU:2, one launch (start us, length us, event | category | flops | bytes accessed | tf_op | source)
XLA Modules:
  0.0 23.9 jit_solution(6604633144086323781)
XLA Ops:
  1.3 21.5 %shard_map.104 = (bf16[512,1536]{1,0:T(8,128)(2,1)S(1)}, bf16[3,16,16,256]{3,2,1,0:T(8,128)(2,1)S(1)}, bf16[64,256]{1,0:T(8,128)(2,1)S(1)}, bf16[64,256]{1,0:T(8,128)(2,1)S(1)}) custom-call(bf16[512,1536]{1,0:T(8,128)(2,1)} %feat_hbm.1, f32[5,1536]{1,0:T(8,128)} %taps_hbm.1, f32[12,128]{1,0:T(8,128)} %bitcast.3, bf16[1536,1536]{1,0:T(8,128)(2,1)} %point_hbm.1, ...), custom_call_target="tpu_custom_call" | custom-call | tf_op jit(solution)/shard_map/pallas_call | solution.py:302
  22.7 1.2 %shard_map.105 = (bf16[512,1536]{1,0:T(8,128)(2,1)}, bf16[64,768]{1,0:T(8,128)(2,1)}) custom-call(bf16[512,1536]{1,0:T(8,128)(2,1)S(1)} %get-tuple-element.6.enc, bf16[3,16,16,256]{3,2,1,0:T(8,128)(2,1)S(1)} %get-tuple-element.7.in_rows, bf16[64,256]{1,0:T(8,128)(2,1)S(1)} %get-tuple-element.8.dhot, bf16[64,256]{1,0:T(8,128)(2,1)S(1)} %get-tuple-element.9.ahot), custom_call_target="tpu_custom_call" | custom-call | tf_op jit(solution)/shard_map/pallas_call | solution.py:358

commit v5 on v4

--- a/solution.py
+++ b/solution.py
@@ -227,51 +227,60 @@
         ask(d).wait()
 
 
+    def hops(d):
+        y, x = divmod(d, side)
+        return min(y, side - y) + min(x, side - x)
+
+    order = sorted(range(n), key=lambda d: -hops(d))
     target = me * CAP + lax.broadcasted_iota(jnp.int32, (CAP, slots), 0)
     place = lax.broadcasted_iota(jnp.int32, (CAP, rows), 1)
-    for s in range(n):
-        d, a = asks[s, 0:1, :], asks[s, 1:2, :]
-        found = jnp.where((d >> 9) == target, (d & (rows - 1)).astype(jnp.float32), 0.0)
-        found += jnp.where((a >> 9) == target, ((a & (rows - 1)) + rows).astype(jnp.float32), 0.0)
-        index = jnp.sum(found, axis=1, keepdims=True).astype(jnp.int32)
-        hot[s * CAP : (s + 1) * CAP, :] = jnp.where(
-            (index & (rows - 1)) == place, 1.0, 0.0
-        ).astype(jnp.bfloat16)
-        kinds[s * CAP : (s + 1) * CAP, :] = jnp.broadcast_to(index, (CAP, LANES))
-
-    for c in range(channels // WIDE):
-        cols = slice(c * WIDE, (c + 1) * WIDE)
-        picked[:, cols] = jnp.dot(
-            hot[...], enc[:, cols], preferred_element_type=jnp.float32
-        ).astype(jnp.bfloat16)
-
-    def send(c, d):
+
+    def send(c, i):
+        d = order[i]
         return pltpu.make_async_remote_copy(
-            out_rows.at[c, peers[d]],
+            out_rows.at[c, i],
             in_rows.at[c, me],
             row_send.at[c, d],
             row_recv.at[c, d],
             device_id={"seq": peers[d]},
         )
 
-    def hops(d):
-        y, x = divmod(d, side)
-        return min(y, side - y) + min(x, side - x)
-
-    order = sorted(range(1, n), key=lambda d: -hops(d))
-    is_accept = jnp.concatenate([kinds[...] >= rows] * (WIDE // LANES), axis=1)
+    group = n // 2
+    for g in range(0, n, group):
+        span = slice(g * CAP, (g + group) * CAP)
+        for i in range(g, g + group):
+            d, a = asks[peers[order[i]], 0:1, :], asks[peers[order[i]], 1:2, :]
+            found = jnp.where((d >> 9) == target, (d & (rows - 1)).astype(jnp.float32), 0.0)
+            found += jnp.where(
+                (a >> 9) == target, ((a & (rows - 1)) + rows).astype(jnp.float32), 0.0
+            )
+            index = jnp.sum(found, axis=1, keepdims=True).astype(jnp.int32)
+            hot[i * CAP : (i + 1) * CAP, :] = jnp.where(
+                (index & (rows - 1)) == place, 1.0, 0.0
+            ).astype(jnp.bfloat16)
+            kinds[i * CAP : (i + 1) * CAP, :] = jnp.broadcast_to(index, (CAP, LANES))
+        for c in range(channels // WIDE):
+            cols = slice(c * WIDE, (c + 1) * WIDE)
+            picked[span, cols] = jnp.dot(
+                hot[span, :], enc[:, cols], preferred_element_type=jnp.float32
+            ).astype(jnp.bfloat16)
+        is_accept = jnp.concatenate([kinds[span, :] >= rows] * (WIDE // LANES), axis=1)
+        for c in range(width // WIDE):
+            cols = slice(c * WIDE, (c + 1) * WIDE)
+            left = jnp.dot(picked[span, :], donor[:, cols], preferred_element_type=jnp.float32)
+            right = jnp.dot(picked[span, :], accept[:, cols], preferred_element_type=jnp.float32)
+            out_rows[c, g : g + group] = (
+                jnp.where(is_accept, right, left).astype(jnp.bfloat16).reshape(group, CAP, WIDE)
+            )
+            for i in range(g, min(g + group, n - 1)):
+                send(c, i).start()
+
     for c in range(width // WIDE):
-        cols = slice(c * WIDE, (c + 1) * WIDE)
-        left = jnp.dot(picked[...], donor[:, cols], preferred_element_type=jnp.float32)
-        right = jnp.dot(picked[...], accept[:, cols], preferred_element_type=jnp.float32)
-        out_rows[c] = jnp.where(is_accept, right, left).astype(jnp.bfloat16).reshape(n, CAP, WIDE)
-        for d in order:
-            send(c, d).start()
-
-    for c in range(width // WIDE):
-        in_rows[c, me] = out_rows[c, me]
-        for d in order:
-            send(c, d).wait()
+        in_rows[c, me] = out_rows[c, n - 1]
+    for g in range(0, n, group):
+        for c in range(width // WIDE):
+            for i in range(g, min(g + group, n - 1)):
+                send(c, i).wait()
 
 
 def finish(enc, in_rows, dhot, ahot, enc_hbm, junc_hbm, junc, sem):

time: 24.1 us -> 23.6 us (0.979)
  Pallas kernels: 22.6 us -> 22.2 us
    pallas_call x1, Pallas kernels: 21.5 us -> 21 us  [on_device(): pl.pallas_call(functools.partial(kernel, side), out_shape=(pltpu.VMEM((ro...]
where the time goes in v5:
time: 23.6 us; the launch traced here: 23.5 us
  Pallas kernels  22.2 us (94%)
  between operations  1.29 us (5%)
    pallas_call x1, Pallas kernels, on_device(): pl.pallas_call(functools.partial(kernel, side), out_shape=(pltpu.VMEM((ro...  21 us
    pallas_call x1, Pallas kernels, on_device(): pl.pallas_call(finish, out_shape=(jax.ShapeDtypeStruct((rows, channels),...  1.19 us

profile of v5, /device:TPU:2, one launch (start us, length us, event | category | flops | bytes accessed | tf_op | source)
XLA Modules:
  0.0 23.5 jit_solution(4659024778880588881)
XLA Ops:
  1.3 21.0 %shard_map.104 = (bf16[512,1536]{1,0:T(8,128)(2,1)S(1)}, bf16[3,16,16,256]{3,2,1,0:T(8,128)(2,1)S(1)}, bf16[64,256]{1,0:T(8,128)(2,1)S(1)}, bf16[64,256]{1,0:T(8,128)(2,1)S(1)}) custom-call(bf16[512,1536]{1,0:T(8,128)(2,1)} %feat_hbm.1, f32[5,1536]{1,0:T(8,128)} %taps_hbm.1, f32[12,128]{1,0:T(8,128)} %bitcast.3, bf16[1536,1536]{1,0:T(8,128)(2,1)} %point_hbm.1, ...), custom_call_target="tpu_custom_call" | custom-call | tf_op jit(solution)/shard_map/pallas_call | solution.py:311
  22.3 1.2 %shard_map.105 = (bf16[512,1536]{1,0:T(8,128)(2,1)}, bf16[64,768]{1,0:T(8,128)(2,1)}) custom-call(bf16[512,1536]{1,0:T(8,128)(2,1)S(1)} %get-tuple-element.6.enc, bf16[3,16,16,256]{3,2,1,0:T(8,128)(2,1)S(1)} %get-tuple-element.7.in_rows, bf16[64,256]{1,0:T(8,128)(2,1)S(1)} %get-tuple-element.8.dhot, bf16[64,256]{1,0:T(8,128)(2,1)S(1)} %get-tuple-element.9.ahot), custom_call_target="tpu_custom_call" | custom-call | tf_op jit(solution)/shard_map/pallas_call | solution.py:367
